TPU v7x, 512 devices: a whole 4x4x16 slice. The times are simulated.
512 devices in a mesh: dp: 128 (over x, z, core), tensor: 4 (over y).
Axes of the slice: x: 4, y: 4, z: 16, core: 2. Of those that a mesh axis runs over, the one named last changes fastest.
Arguments:
- tokens: bfloat16 [32768, 2048], P('dp', 'tensor'), may hold values from -6 to 6
- expert_ids: int32 [32768, 2], P('dp'), may hold values from 0 to 127, as said below
- route_weights: float32 [32768, 2], P('dp'), may hold values from 0.2 to 1
- gate_weight: bfloat16 [128, 2048, 1024], P('dp', None, 'tensor'), may hold values from -0.125 to 0.125
- up_weight: bfloat16 [128, 2048, 1024], P('dp', None, 'tensor'), may hold values from -0.125 to 0.125
- down_weight: bfloat16 [128, 1024, 2048], P('dp', 'tensor'), may hold values from -0.1875 to 0.1875
Outputs:
- moe_out: bfloat16 [32768, 2048], P('dp', 'tensor')
Inputs may be any that keep to these rules, and one draw needn't show every extreme that they name: `expert_ids`: the two experts of a row differ. Among the rows of one index of dp, no expert is named more than 8 times.
All inputs are finite; a program needn't handle non-finite values.
Results may differ from a plain program's by a relative error of at most 0.011.
Values may be sent and summed in bfloat16 or wider, within the bound.
A program may use at most 64 MiB of HBM per device.

v0:
```python
import jax
import jax.numpy as jnp
from jax import lax
from jax.sharding import PartitionSpec as P


def body(tokens, expert_ids, route_weights, gate_weight, up_weight, down_weight):
    tok_count = tokens.shape[0]
    local_experts = gate_weight.shape[0]
    model_width = gate_weight.shape[1]
    groups = lax.axis_size("dp")
    experts_all = local_experts * groups
    capacity = 4 * tok_count // groups
    chosen = expert_ids.reshape(-1)
    onehot = (chosen[:, None] == jnp.arange(experts_all, dtype=jnp.int32)[None, :]).astype(
        jnp.int32
    )
    earlier = jnp.cumsum(onehot, axis=0) - onehot
    slot_index = jnp.sum(earlier * onehot, axis=1)
    flat_slot = chosen * capacity + slot_index
    source_rows = tokens[jnp.arange(chosen.shape[0], dtype=jnp.int32) // 2]
    send_buffer = (
        jnp.zeros((experts_all * capacity, tokens.shape[1]), jnp.bfloat16)
        .at[flat_slot]
        .set(source_rows)
    )
    send_buffer = send_buffer.reshape(experts_all, 1, capacity, tokens.shape[1])
    features = lax.all_gather(
        lax.all_to_all(send_buffer, "dp", split_axis=0, concat_axis=1, tiled=True),
        "tensor",
        axis=3,
        tiled=True,
    )
    slot_count = features.shape[2]
    token_rows = features[0].reshape(-1, model_width)
    gate_value = jnp.dot(token_rows, gate_weight[0], preferred_element_type=jnp.float32)
    up_value = jnp.dot(token_rows, up_weight[0], preferred_element_type=jnp.float32)
    hidden = (jax.nn.silu(gate_value) * up_value).astype(jnp.bfloat16)
    partial_sum = jnp.dot(hidden, down_weight[0], preferred_element_type=jnp.float32)
    results = [partial_sum.reshape(features.shape[1], slot_count, model_width)]
    partial_out = jnp.stack(results, axis=0)
    reduced = lax.psum_scatter(
        partial_out.astype(jnp.bfloat16), "tensor", scatter_dimension=3, tiled=True
    )
    came_back = lax.all_to_all(reduced, "dp", split_axis=1, concat_axis=0, tiled=True)
    quarter_width = came_back.shape[3]
    result_table = came_back.reshape(experts_all * capacity, quarter_width)
    picked = result_table[flat_slot].astype(jnp.float32).reshape(tok_count, 2, quarter_width)
    mixed_out = jnp.sum(picked * route_weights[:, :, None], axis=1)
    return mixed_out.astype(jnp.bfloat16)


def solution(mesh):
    return jax.shard_map(
        body,
        mesh=mesh,
        in_specs=(
            P("dp", "tensor"),
            P("dp", None),
            P("dp", None),
            P("dp", None, "tensor"),
            P("dp", None, "tensor"),
            P("dp", "tensor", None),
        ),
        out_specs=P("dp", "tensor"),
        check_vma=False,
    )
```

profile of v0, /device:TPU:2, one launch (start us, length us, event | category | flops | bytes accessed | tf_op | source)
XLA Modules:
  0.0 289.4 jit_solution(14001448226767223536)
XLA Ops:
  6.5 0.0 copy-start
  6.5 0.0 copy-start.3
  6.5 0.0 all-gather.3.cloned.1.call-start
  6.5 1.0 copy.18
  7.5 0.1 eq.29
  7.7 0.1 eq.25
  7.8 0.7 broadcast_multiply_fusion
  8.5 0.1 copy.20
  8.6 0.2 fusion.22
  8.9 0.1 copy.17
  9.1 0.1 mul.36
  9.2 0.2 fusion.21
  9.5 6.4 %scatter_custom_fusion = bf16[1024,512]{1,0:T(8,128)(2,1)S(1)} fusion(s32[512]{0:T(512)S(1)} %bitcast.49, bf16[256,512]{1,0:T(8,128)(2,1)} %param.6, s32[1024]{0:T(1024)S(1)} %pad_clamp_fusion.1, bf16[]{:T(256)} %constant.26.clone.1), kind=kCustom, calls=%fused_computation.16 | custom fusion | bytes 1049088 | tf_op jit(solution)/shard_map/scatter | solution.py:25
  15.9 75.5 %all_to_all.21 = bf16[128,1,8,512]{3,2,1,0:T(8,128)(2,1)} all-to-all(bf16[128,1,8,512]{3,2,1,0:T(8,128)(2,1)S(1)} %bitcast.44), channel_id=1, replica_groups=mesh['dp'=128,'tensor'=4] {'dp'}, dimensions={0} | all-to-all | bytes 2097152 | tf_op jit(solution)/shard_map/all_to_all | solution.py:29
  91.4 0.0 copy-start.4
  91.4 0.0 all-gather.3.cloned.1.call-update
  91.4 0.2 reduce-scatter.2.cloned.1.call-start
  91.7 47.5 %all-gather.3.cloned.1.call-done = bf16[128,1,8,2048]{3,2,1,0:T(8,128)(2,1)} async-done(((bf16[128,1,8,512]{3,2,1,0:T(8,128)(2,1)}), bf16[128,1,8,2048]{3,2,1,0:T(8,128)(2,1)}) %all-gather.3.cloned.1.call-update) | async-done | bytes 4194320 | tf_op jit(solution)/shard_map/all_gather | solution.py:28
  139.2 0.0 copy-done.3
  139.2 0.0 copy-start.2
  139.2 3.6 %fusion.2 = f32[1024,256]{1,0:T(8,128)S(1)} fusion(bf16[128,1,8,2048]{3,2,1,0:T(8,128)(2,1)} %all-gather.3.cloned.1.call-done, bf16[1,2048,256]{2,1,0:T(8,128)(2,1)S(1)} %copy-done.3), kind=kOutput, calls=%fused_computation.5 | convolution fusion | flops 1073741824 | bytes 6291456 | tf_op jit(solution)/shard_map/dot_general | solution.py:36
  142.8 0.0 copy-done.4
  142.8 0.0 copy-done.2
  142.8 1.3 fusion.10
  144.1 0.0 copy-done
  144.1 3.2 %convert_bitcast_fusion = bf16[1,128,8,2048]{3,1,2,0:T(8,128)(2,1)} fusion(bf16[1,256,2048]{2,1,0:T(8,128)(2,1)S(1)} %copy-done, bf16[128,8,256]{2,1,0:T(8,128)(2,1)S(1)} %fusion.10), kind=kOutput, calls=%fused_computation.7 | convolution fusion | flops 1075838976 | bytes 5767168 | tf_op jit(solution)/shard_map/dot_general | solution.py:39
  147.3 0.0 copy-start.1
  147.3 0.0 reduce-scatter.2.cloned.1.call-update
  147.4 55.1 %reduce-scatter.2.cloned.1.call-done = bf16[1,128,8,512]{3,1,2,0:T(8,128)(2,1)} async-done(((bf16[1,128,8,2048]{3,1,2,0:T(8,128)(2,1)}), bf16[1,128,8,512]{3,1,2,0:T(8,128)(2,1)}) %reduce-scatter.2.cloned.1.call-update) | async-done | bytes 1048592 | tf_op jit(solution)/shard_map/reduce_scatter | solution.py:42
  202.4 2.8 copy.23
  205.2 16.6 %all-to-all-start.1 = ((bf16[1,128,8,512]{3,2,0,1:T(8,128)(2,1)}), bf16[1,128,8,512]{3,2,0,1:T(8,128)(2,1)S(1)}, u32[]{:S(2)}, u32[]{:S(2)}) async-start(bf16[1,128,8,512]{3,2,0,1:T(8,128)(2,1)} %copy.23), calls=%async_computation.2 | async-start | bytes 2097152 | tf_op jit(solution)/shard_map/all_to_all | solution.py:45
  221.8 0.0 copy-done.1
  221.8 0.1 copy.24
  222.0 55.9 %all-to-all-done.1 = bf16[1,128,8,512]{3,2,0,1:T(8,128)(2,1)S(1)} async-done(((bf16[1,128,8,512]{3,2,0,1:T(8,128)(2,1)}), bf16[1,128,8,512]{3,2,0,1:T(8,128)(2,1)S(1)}, u32[]{:S(2)}, u32[]{:S(2)}) %all-to-all-start.1) | async-done | bytes 1048608 | tf_op jit(solution)/shard_map/all_to_all | solution.py:45
  277.9 2.0 gather_fusion
  279.9 0.7 reshape.113
  280.5 2.1 multiply_reduce_fusion
  (10 shorter events, 0.1 us)
Async XLA Ops:
  6.5 137.6 %copy-start = (bf16[1,256,2048]{2,1,0:T(8,128)(2,1)S(1)}, bf16[1,256,2048]{2,1,0:T(8,128)(2,1)}, u32[]{:S(2)}) copy-start(bf16[1,256,2048]{2,1,0:T(8,128)(2,1)} %param.11) | copy-start | bytes 3145732
  6.5 132.7 %copy-start.3 = (bf16[1,2048,256]{2,1,0:T(8,128)(2,1)S(1)}, bf16[1,2048,256]{2,1,0:T(8,128)(2,1)}, u32[]{:S(2)}) copy-start(bf16[1,2048,256]{2,1,0:T(8,128)(2,1)} %param.9) | copy-start | bytes 3145732
  6.5 132.7 %all-gather.3.cloned.1.call-start = ((), (), s32[]{:S(2)}) async-start(), calls=%async_computation.4 | async-start | bytes 5242880 | tf_op jit(solution)/shard_map/all_gather | solution.py:28
  91.4 51.4 %copy-start.4 = (bf16[1,2048,256]{2,1,0:T(8,128)(2,1)S(1)}, bf16[1,2048,256]{2,1,0:T(8,128)(2,1)}, u32[]{:S(2)}) copy-start(bf16[1,2048,256]{2,1,0:T(8,128)(2,1)} %param.10) | copy-start | bytes 3145732
  91.4 111.0 %reduce-scatter.2.cloned.1.call-start = ((), (), s32[]{:S(2)}) async-start(), calls=%async_computation.3 | async-start | bytes 5242880 | tf_op jit(solution)/shard_map/reduce_scatter | solution.py:42
  139.2 3.6 %copy-start.2 = (bf16[128,1,8,2048]{3,2,1,0:T(8,128)(2,1)S(1)}, bf16[128,1,8,2048]{3,2,1,0:T(8,128)(2,1)}, u32[]{:S(2)}) copy-start(bf16[128,1,8,2048]{3,2,1,0:T(8,128)(2,1)} %all-gather.3.cloned.1.call-done) | copy-start | bytes 12582916
  147.3 74.5 %copy-start.1 = (f32[256,2]{0,1:T(2,128)S(1)}, f32[256,2]{0,1:T(2,128)}, u32[]{:S(2)}) copy-start(f32[256,2]{0,1:T(2,128)} %param.8) | copy-start | bytes 6148
  205.2 72.7 %all-to-all-start.1 = ((bf16[1,128,8,512]{3,2,0,1:T(8,128)(2,1)}), bf16[1,128,8,512]{3,2,0,1:T(8,128)(2,1)S(1)}, u32[]{:S(2)}, u32[]{:S(2)}) async-start(bf16[1,128,8,512]{3,2,0,1:T(8,128)(2,1)} %copy.23), calls=%async_computation.2 | async-start | bytes 2097152 | tf_op jit(solution)/shard_map/all_to_all | solution.py:45
Sparse Core Ops, SparseCore 0:
  91.6 47.6 all-gather.2
  147.5 54.8 reduce-scatter.1
where the time goes:
time: 290 us; the launch traced here: 289 us
  waiting for transfers between devices  159 us (55%)
  blocking collectives  75.5 us (26%)
  starting transfers between devices  16.8 us (6%)
  local copies, waits for them, and re-layouts  13.6 us (5%)
  between operations  13.6 us (5%)
  matrix products  8.07 us (3%)
  other arithmetic  3.26 us (1%)
    all_to_all x1, blocking collectives, body(): lax.all_to_all(send_buffer, 'dp', split_axis=0, concat_axis=1, tiled=True)  75.5 us
    all_to_all x1, waiting for transfers between devices, body(): lax.all_to_all(reduced, 'dp', split_axis=1, concat_axis=0, tiled=True)  55.9 us
    reduce_scatter x1, waiting for transfers between devices, body(): lax.psum_scatter(partial_out.astype(jnp.bfloat16), 'tensor', scatter_dime...  55.1 us
    all_gather x1, waiting for transfers between devices, body(): lax.all_gather(lax.all_to_all(send_buffer, 'dp', split_axis=0, concat_axi...  47.5 us
    all_to_all x1, starting transfers between devices, body(): lax.all_to_all(reduced, 'dp', split_axis=1, concat_axis=0, tiled=True)  16.6 us
    scatter x1, local copies, waits for them, and re-layouts, body(): send_buffer = jnp.zeros((experts_all * capacity, tokens.shape[1]), jnp.bf...  6.4 us
  transfers between devices with their start and end apart: 3, of which 3 were waited for; matrix products, arithmetic and copies ran while one was open for 0% of the time, Pallas kernels for 0%

commit v1 on v0

--- a/solution.py
+++ b/solution.py
@@ -25,12 +25,17 @@
         .set(source_rows)
     )
     send_buffer = send_buffer.reshape(experts_all, 1, capacity, tokens.shape[1])
-    features = lax.all_gather(
-        lax.all_to_all(send_buffer, "dp", split_axis=0, concat_axis=1, tiled=True),
-        "tensor",
-        axis=3,
-        tiled=True,
-    )
+    array = lax.all_to_all(send_buffer, "dp", split_axis=0, concat_axis=1, tiled=True)
+    ways = lax.axis_size("tensor")
+    up = [(d, (d + 1) % ways) for d in range(ways)]
+    down = [(d, (d - 1) % ways) for d in range(ways)]
+    earlier_2, later = ([array], [array])
+    for _ in range(ways // 2):
+        earlier_2.append(lax.ppermute(earlier_2[-1], "tensor", up))
+    for _ in range((ways - 1) // 2):
+        later.append(lax.ppermute(later[-1], "tensor", down))
+    line = jnp.concatenate([*earlier_2[::-1], *later[1:]], axis=3)
+    features = jnp.roll(line, (lax.axis_index("tensor") - ways // 2) * array.shape[3], axis=3)
     slot_count = features.shape[2]
     token_rows = features[0].reshape(-1, model_width)
     gate_value = jnp.dot(token_rows, gate_weight[0], preferred_element_type=jnp.float32)

time: 290 us -> 292 us (level)
  waiting for transfers between devices: 159 us -> 147 us
  starting transfers between devices: 16.8 us -> 27.3 us
  local copies, waits for them, and re-layouts: 13.6 us -> 19.4 us
    all_gather x1 -> x0, waiting for transfers between devices: 47.5 us -> none  [body(): lax.all_gather(lax.all_to_all(send_buffer, 'dp', split_axis=0, concat_axi...]
    ppermute x0 -> x3, waiting for transfers between devices: none -> 40.9 us  [the longest x2 40.9 us: body(): earlier_2.append(lax.ppermute(earlier_2[-1], 'tensor', up))]
    ppermute x0 -> x3, starting transfers between devices: none -> 10.7 us  [the longest x2 5.67 us: body(): earlier_2.append(lax.ppermute(earlier_2[-1], 'tensor', up))]
    reduce_scatter x1, waiting for transfers between devices: 55.1 us -> 49.8 us  [body(): lax.psum_scatter(partial_out.astype(jnp.bfloat16), 'tensor', scatter_dime...]
    unnamed x13 -> x18, local copies, waits for them, and re-layouts: 1.11 us -> 5.59 us
  transfers between devices with their start and end apart: 3 -> 5, of which waited for: 3 -> 4; matrix products, arithmetic and copies ran while one was open for 0% -> 1% of each run, Pallas kernels for 0% -> 0%
where the time goes in v1:
time: 292 us
  waiting for transfers between devices  147 us (50%)
  blocking collectives  75.4 us (26%)
  starting transfers between devices  27.3 us (9%)
  local copies, waits for them, and re-layouts  19.4 us (7%)
  between operations  13.7 us (5%)
  matrix products  5.76 us (2%)
  other arithmetic  3.35 us (1%)
    all_to_all x1, blocking collectives, body(): lax.all_to_all(send_buffer, 'dp', split_axis=0, concat_axis=1, tiled=True)  75.4 us
    all_to_all x1, waiting for transfers between devices, body(): lax.all_to_all(reduced, 'dp', split_axis=1, concat_axis=0, tiled=True)  55.9 us
    reduce_scatter x1, waiting for transfers between devices, body(): lax.psum_scatter(partial_out.astype(jnp.bfloat16), 'tensor', scatter_dime...  49.8 us
    ppermute x2, waiting for transfers between devices, body(): earlier_2.append(lax.ppermute(earlier_2[-1], 'tensor', up))  40.9 us
    all_to_all x1, starting transfers between devices, body(): lax.all_to_all(reduced, 'dp', split_axis=1, concat_axis=0, tiled=True)  16.6 us
    scatter x1, local copies, waits for them, and re-layouts, body(): send_buffer = jnp.zeros((experts_all * capacity, tokens.shape[1]), jnp.bf...  6.4 us
  transfers between devices with their start and end apart: 5, of which 4 were waited for; matrix products, arithmetic and copies ran while one was open for 1% of the time, Pallas kernels for 0%

profile of v1, /device:TPU:2, one launch (start us, length us, event | category | flops | bytes accessed | tf_op | source)
XLA Modules:
  0.0 291.6 jit_solution(2963404168099760652)
XLA Ops:
  6.5 0.0 copy-start
  6.5 0.0 reduce-scatter.2.cloned.1.call-start
  6.5 0.8 broadcast_multiply_fusion
  7.3 0.8 copy.18
  8.1 0.1 eq.32
  8.3 0.1 eq.28
  8.4 0.1 copy.17
  8.6 0.1 mul.39
  8.7 0.1 copy.20
  8.8 0.2 fusion.16
  9.2 0.2 fusion.15
  9.4 6.4 %scatter_custom_fusion = bf16[1024,512]{1,0:T(8,128)(2,1)S(1)} fusion(s32[512]{0:T(512)S(1)} %bitcast.52, bf16[256,512]{1,0:T(8,128)(2,1)} %param.6, s32[1024]{0:T(1024)S(1)} %pad_clamp_fusion.1, bf16[]{:T(256)} %constant.49.clone.1), kind=kCustom, calls=%fused_computation.16 | custom fusion | bytes 1049088 | tf_op jit(solution)/shard_map/scatter | solution.py:25
  15.8 75.4 %all_to_all.21 = bf16[128,1,8,512]{3,2,1,0:T(8,128)(2,1)S(1)} all-to-all(bf16[128,1,8,512]{3,2,1,0:T(8,128)(2,1)S(1)} %bitcast.47), channel_id=1, replica_groups=mesh['dp'=128,'tensor'=4] {'dp'}, dimensions={0} | all-to-all | bytes 2097152 | tf_op jit(solution)/shard_map/all_to_all | solution.py:28
  91.2 3.5 %collective-permute-start = (bf16[1,128,8,512]{3,2,1,0:T(8,128)(2,1)S(1)}, bf16[1,128,8,512]{3,2,1,0:T(8,128)(2,1)S(1)}, u32[]{:S(2)}, u32[]{:S(2)}) collective-permute-start(bf16[1,128,8,512]{3,2,1,0:T(8,128)(2,1)S(1)} %bitcast.45), channel_id=1, source_target_pairs={{0,1},{1,2},{2,3},{3,0},{4,5},{5,6},{6,7},{7,4},{8,9},{9,10},{10,1... | collective-permute-start | bytes 3145736 | tf_op jit(solution)/shard_map/ppermute | solution.py:34
  94.7 22.8 %collective-permute-done = bf16[1,128,8,512]{3,2,1,0:T(8,128)(2,1)S(1)} collective-permute-done((bf16[1,128,8,512]{3,2,1,0:T(8,128)(2,1)S(1)}, bf16[1,128,8,512]{3,2,1,0:T(8,128)(2,1)S(1)}, u32[]{:S(2)}, u32[]{:S(2)}) %collective-permute-start) | collective-permute-done | bytes 1048608 | tf_op jit(solution)/shard_map/ppermute | solution.py:34
  117.5 2.2 collective-permute-start.1
  119.7 5.0 %collective-permute-start.2 = (bf16[1,128,8,512]{3,2,1,0:T(8,128)(2,1)S(1)}, bf16[1,128,8,512]{3,2,1,0:T(8,128)(2,1)}, u32[]{:S(2)}, u32[]{:S(2)}) collective-permute-start(bf16[1,128,8,512]{3,2,1,0:T(8,128)(2,1)S(1)} %bitcast.46), channel_id=1, source_target_pairs={{0,3},{1,0},{2,1},{3,2},{4,7},{5,4},{6,5},{7,6},{8,11},{9,8},{10,9... | collective-permute-start | bytes 3145736 | tf_op jit(solution)/shard_map/ppermute | solution.py:36
  124.8 0.0 copy-start.2
  124.8 18.2 %collective-permute-done.1 = bf16[1,128,8,512]{3,2,1,0:T(8,128)(2,1)} collective-permute-done((bf16[1,128,8,512]{3,2,1,0:T(8,128)(2,1)S(1)}, bf16[1,128,8,512]{3,2,1,0:T(8,128)(2,1)}, u32[]{:S(2)}, u32[]{:S(2)}) %collective-permute-start.1) | collective-permute-done | bytes 1048608 | tf_op jit(solution)/shard_map/ppermute | solution.py:34
  142.9 1.3 constant_dynamic-update-slice_fusion.7
  144.3 0.1 constant_dynamic-update-slice_fusion.6
  144.4 0.1 constant_dynamic-update-slice_fusion.5
  144.5 0.0 collective-permute-done.2
  144.6 1.3 constant_dynamic-update-slice_fusion.4
  145.9 0.0 copy-start.3
  145.9 1.4 constant_dynamic-update-slice_fusion.3
  147.4 0.1 constant_dynamic-update-slice_fusion.2
  147.5 0.1 constant_dynamic-update-slice_fusion.1
  147.6 1.3 constant_dynamic-update-slice_fusion
  149.0 0.0 copy-done.2
  149.0 1.3 fusion.2
  150.3 0.0 copy-done.3
  150.3 1.3 fusion.13
  151.6 0.0 copy-done
  151.6 0.0 copy-start.1
  151.6 3.2 %convert_bitcast_fusion = bf16[1,128,8,2048]{3,1,2,0:T(8,128)(2,1)} fusion(bf16[1,256,2048]{2,1,0:T(8,128)(2,1)S(1)} %copy-done, bf16[128,8,256]{2,1,0:T(8,128)(2,1)S(1)} %fusion.13), kind=kOutput, calls=%fused_computation.7 | convolution fusion | flops 1075838976 | bytes 5767168 | tf_op jit(solution)/shard_map/dot_general | solution.py:44
  154.8 0.0 reduce-scatter.2.cloned.1.call-update
  154.8 49.8 %reduce-scatter.2.cloned.1.call-done = bf16[1,128,8,512]{3,1,2,0:T(8,128)(2,1)} async-done(((bf16[1,128,8,2048]{3,1,2,0:T(8,128)(2,1)}), bf16[1,128,8,512]{3,1,2,0:T(8,128)(2,1)}) %reduce-scatter.2.cloned.1.call-update) | async-done | bytes 1048592 | tf_op jit(solution)/shard_map/reduce_scatter | solution.py:47
  204.6 2.8 copy.23
  207.4 16.6 %all-to-all-start.1 = ((bf16[1,128,8,512]{3,2,0,1:T(8,128)(2,1)}), bf16[1,128,8,512]{3,2,0,1:T(8,128)(2,1)S(1)}, u32[]{:S(2)}, u32[]{:S(2)}) async-start(bf16[1,128,8,512]{3,2,0,1:T(8,128)(2,1)} %copy.23), calls=%async_computation.2 | async-start | bytes 2097152 | tf_op jit(solution)/shard_map/all_to_all | solution.py:50
  224.0 0.0 copy-done.1
  224.0 0.1 copy.24
  224.2 55.9 %all-to-all-done.1 = bf16[1,128,8,512]{3,2,0,1:T(8,128)(2,1)S(1)} async-done(((bf16[1,128,8,512]{3,2,0,1:T(8,128)(2,1)}), bf16[1,128,8,512]{3,2,0,1:T(8,128)(2,1)S(1)}, u32[]{:S(2)}, u32[]{:S(2)}) %all-to-all-start.1) | async-done | bytes 1048608 | tf_op jit(solution)/shard_map/all_to_all | solution.py:50
  280.1 2.0 gather_fusion
  282.1 0.7 reshape.113
  282.8 2.1 multiply_reduce_fusion
  (10 shorter events, 0.1 us)
Async XLA Ops:
  6.5 145.1 %copy-start = (bf16[1,256,2048]{2,1,0:T(8,128)(2,1)S(1)}, bf16[1,256,2048]{2,1,0:T(8,128)(2,1)}, u32[]{:S(2)}) copy-start(bf16[1,256,2048]{2,1,0:T(8,128)(2,1)} %param.11) | copy-start | bytes 3145732
  6.5 198.1 %reduce-scatter.2.cloned.1.call-start = ((), (), s32[]{:S(2)}) async-start(), calls=%async_computation.3 | async-start | bytes 5242880 | tf_op jit(solution)/shard_map/reduce_scatter | solution.py:47
  91.2 26.2 %collective-permute-start = (bf16[1,128,8,512]{3,2,1,0:T(8,128)(2,1)S(1)}, bf16[1,128,8,512]{3,2,1,0:T(8,128)(2,1)S(1)}, u32[]{:S(2)}, u32[]{:S(2)}) collective-permute-start(bf16[1,128,8,512]{3,2,1,0:T(8,128)(2,1)S(1)} %bitcast.45), channel_id=1, source_target_pairs={{0,1},{1,2},{2,3},{3,0},{4,5},{5,6},{6,7},{7,4},{8,9},{9,10},{10,1... | collective-permute-start | bytes 3145736 | tf_op jit(solution)/shard_map/ppermute | solution.py:34
  117.5 25.4 %collective-permute-start.1 = (bf16[1,128,8,512]{3,2,1,0:T(8,128)(2,1)S(1)}, bf16[1,128,8,512]{3,2,1,0:T(8,128)(2,1)}, u32[]{:S(2)}, u32[]{:S(2)}) collective-permute-start(bf16[1,128,8,512]{3,2,1,0:T(8,128)(2,1)S(1)} %collective-permute-done), channel_id=1, source_target_pairs={{0,1},{1,2},{2,3},{3,0},{4,5},{5,6},{6,7},{7,4},{8,9},{9,10},{10,1... | collective-permute-start | bytes 3145736 | tf_op jit(solution)/shard_map/ppermute | solution.py:34
  119.7 24.9 %collective-permute-start.2 = (bf16[1,128,8,512]{3,2,1,0:T(8,128)(2,1)S(1)}, bf16[1,128,8,512]{3,2,1,0:T(8,128)(2,1)}, u32[]{:S(2)}, u32[]{:S(2)}) collective-permute-start(bf16[1,128,8,512]{3,2,1,0:T(8,128)(2,1)S(1)} %bitcast.46), channel_id=1, source_target_pairs={{0,3},{1,0},{2,1},{3,2},{4,7},{5,4},{6,5},{7,6},{8,11},{9,8},{10,9... | collective-permute-start | bytes 3145736 | tf_op jit(solution)/shard_map/ppermute | solution.py:36
  124.8 24.2 %copy-start.2 = (bf16[1,2048,256]{2,1,0:T(8,128)(2,1)S(1)}, bf16[1,2048,256]{2,1,0:T(8,128)(2,1)}, u32[]{:S(2)}) copy-start(bf16[1,2048,256]{2,1,0:T(8,128)(2,1)} %param.9) | copy-start | bytes 3145732
  145.9 4.4 %copy-start.3 = (bf16[1,2048,256]{2,1,0:T(8,128)(2,1)S(1)}, bf16[1,2048,256]{2,1,0:T(8,128)(2,1)}, u32[]{:S(2)}) copy-start(bf16[1,2048,256]{2,1,0:T(8,128)(2,1)} %param.10) | copy-start | bytes 3145732
  151.6 72.4 %copy-start.1 = (f32[256,2]{0,1:T(2,128)S(1)}, f32[256,2]{0,1:T(2,128)}, u32[]{:S(2)}) copy-start(f32[256,2]{0,1:T(2,128)} %param.8) | copy-start | bytes 6148
  207.4 72.7 %all-to-all-start.1 = ((bf16[1,128,8,512]{3,2,0,1:T(8,128)(2,1)}), bf16[1,128,8,512]{3,2,0,1:T(8,128)(2,1)S(1)}, u32[]{:S(2)}, u32[]{:S(2)}) async-start(bf16[1,128,8,512]{3,2,0,1:T(8,128)(2,1)} %copy.23), calls=%async_computation.2 | async-start | bytes 2097152 | tf_op jit(solution)/shard_map/all_to_all | solution.py:50
Sparse Core Ops, SparseCore 0:
  154.9 49.6 reduce-scatter.1
